TPU v7x, 128 devices: a whole 4x4x4 slice. The times are simulated.
128 devices in a mesh: rep: 8 (over y, z_hi), fsdp: 16 (over x, z_lo, core).
Axes of the slice: x: 4, y: 4, z: 4 (z_hi: 2, z_lo: 2; z = z_hi * 2 + z_lo), core: 2. Of those that a mesh axis runs over, the one named last changes fastest.
Arguments:
- tokens: bfloat16 [65536, 8192], P(('rep', 'fsdp')), may hold values from -6 to 6
- gain: float32 [8192], replicated, may hold values from 0.5 to 1.5
- value_weight: bfloat16 [8, 8192, 1024], P('rep', 'fsdp'), may hold values from -0.0625 to 0.0625
- cotangent: bfloat16 [65536, 1024], P(('rep', 'fsdp')), may hold values from -3 to 3
- codes: bfloat16 [8, 8192, 1024], P('rep', 'fsdp'), may hold values from -4 to 4
- scales: bfloat16 [8, 8192, 8], P('rep', 'fsdp'), may hold values from 0.049804688 to 0.5
- local_frag: bfloat16 [8, 8192, 1024], P('rep', 'fsdp'), may hold values from -6 to 6
- momentum: float32 [8192, 1024], P('fsdp', 'rep'), may hold values from -3 to 3
- global_frag: float32 [8192, 1024], P('fsdp', 'rep'), may hold values from -6 to 6
Outputs:
- values_out: bfloat16 [65536, 1024], P(('rep', 'fsdp'))
- token_gradient: bfloat16 [65536, 8192], P(('rep', 'fsdp'))
- weight_grad: bfloat16 [8, 8192, 1024], P('rep', 'fsdp')
- merged_frag: bfloat16 [8, 8192, 1024], P('rep', 'fsdp')
- new_momentum: float32 [8192, 1024], P('fsdp', 'rep')
- new_global: float32 [8192, 1024], P('fsdp', 'rep')
All inputs are finite; a program needn't handle non-finite values.
Results may differ from a plain program's by a relative error of at most 0.022.
Values may be sent and summed in bfloat16 or wider, within the bound.
No kernel may reach another device: no remote copies, remote signals or barrier semaphores. Data moves between devices by JAX's collectives and lax.ppermute only.
A program may use at most 192 MiB of HBM per device.

v0:
```python
import jax
import jax.numpy as jnp
from jax import lax
from jax.sharding import PartitionSpec as P


def per_device(
    tokens, gain, value_weight, cotangent, codes, scales, local_frag, momentum, global_frag
):
    token_input = tokens.astype(jnp.float32)
    inverse_root_mean = 1.0 / jnp.sqrt(
        jnp.mean(token_input * token_input, axis=-1, keepdims=True) + 1e-05
    )
    centered_tokens = token_input * inverse_root_mean
    normalized_input = (centered_tokens * gain).astype(jnp.bfloat16)
    weight = value_weight[0]
    groups = lax.axis_size("fsdp")
    contract = (((1,), (1,)), ((), ()))
    piece = lax.all_gather(weight, "fsdp", axis=0, tiled=True)
    columns = normalized_input
    outs = jnp.dot(columns, piece, preferred_element_type=jnp.float32)
    back = lax.dot_general(cotangent, piece, contract, preferred_element_type=jnp.float32)
    outs, normed_grad = (outs, back)
    columns = normalized_input
    term = lax.dot_general(
        columns, cotangent, (((0,), (0,)), ((), ())), preferred_element_type=jnp.float32
    )
    summed = lax.psum_scatter(
        (term / groups).astype(jnp.bfloat16), "fsdp", scatter_dimension=0, tiled=True
    )
    values_out = outs.astype(jnp.bfloat16)
    norm_gain = normed_grad * gain
    token_gradient = (
        inverse_root_mean
        * (
            norm_gain
            - centered_tokens * jnp.mean(norm_gain * centered_tokens, axis=-1, keepdims=True)
        )
    ).astype(jnp.bfloat16)
    weight_grad = summed[None]
    replicas = lax.axis_size("rep")
    frag_rows = codes.shape[1]
    block = codes.shape[2] // scales.shape[2]
    block_groups = scales.shape[2]
    delta = (
        codes[0].astype(jnp.float32).reshape(frag_rows, block_groups, block)
        * scales[0].astype(jnp.float32)[..., None]
    ).reshape(frag_rows, block_groups * block)
    average = (
        lax.psum_scatter(delta.astype(jnp.bfloat16), "rep", scatter_dimension=1, tiled=True).astype(
            jnp.float32
        )
        / replicas
    )
    new_momentum = 0.9 * momentum + average
    new_global = global_frag - 0.7 * (average + 0.9 * new_momentum)
    full_global = lax.all_gather(new_global.astype(jnp.bfloat16), "rep", axis=1, tiled=True).astype(
        new_global.dtype
    )
    merged_frag = (0.5 * local_frag[0].astype(jnp.float32) + 0.5 * full_global).astype(
        jnp.bfloat16
    )[None]
    return (values_out, token_gradient, weight_grad, merged_frag, new_momentum, new_global)


def solution(mesh):
    return jax.shard_map(
        per_device,
        mesh=mesh,
        in_specs=(
            P(("rep", "fsdp"), None),
            P(),
            P("rep", "fsdp", None),
            P(("rep", "fsdp"), None),
            P("rep", "fsdp", None),
            P("rep", "fsdp", None),
            P("rep", "fsdp", None),
            P("fsdp", "rep"),
            P("fsdp", "rep"),
        ),
        out_specs=(
            P(("rep", "fsdp"), None),
            P(("rep", "fsdp"), None),
            P("rep", "fsdp", None),
            P("rep", "fsdp", None),
            P("fsdp", "rep"),
            P("fsdp", "rep"),
        ),
        check_vma=False,
    )
```

profile of v0, /device:TPU:6, one launch (start us, length us, event | category | flops | bytes accessed | tf_op | source)
XLA Modules:
  0.0 415.7 jit_solution(8828256702931399827)
XLA Ops:
  7.2 0.0 copy-start
  7.2 0.0 copy-start.3
  7.2 0.0 reduce-scatter.7.cloned.1.call-start
  7.2 0.8 bitcast_convert_fusion
  8.0 0.1 copy.16
  8.1 0.6 mul.79
  8.8 1.8 fusion.15
  10.6 1.3 copy.17
  11.9 0.0 reduce-scatter.7.cloned.1.call-update
  11.9 0.0 all-gather.4.cloned.1.call-start
  12.0 74.7 %reduce-scatter.7.cloned.1.call-done = bf16[128,512]{1,0:T(8,128)(2,1)} async-done(((bf16[1024,512]{1,0:T(8,128)(2,1)}), bf16[128,512]{1,0:T(8,128)(2,1)}) %reduce-scatter.7.cloned.1.call-update) | async-done | bytes 131088
  86.7 1.0 copy.18
  87.7 1.9 fusion.24
  89.7 0.0 all-gather.4.cloned.1.call-update
  89.7 0.0 all-gather.6.cloned.1.call-start
  89.7 0.7 all-gather.6.cloned.1.call-update
  90.4 0.0 reduce-scatter.5.cloned.1.call-start
  90.5 5.1 %fusion.8 = f32[512]{0:T(512)S(1)} fusion(bf16[512,8192]{1,0:T(8,128)(2,1)} %param.9), kind=kLoop, calls=%fused_computation.11 | loop fusion | flops 12582400 | bytes 8390656 | tf_op jit(solution)/shard_map/reduce_sum | solution.py:12
  95.6 0.0 copy-done
  95.6 0.0 copy-done.3
  95.6 16.5 %multiply_convert_fusion = bf16[8192,1024]{1,0:T(8,128)(2,1)} fusion(bf16[512,1024]{1,0:T(8,128)(2,1)S(1)} %copy-done, bf16[512,8192]{1,0:T(8,128)(2,1)} %param.9, f32[8192]{0:T(1024)S(1)} %copy-done.3, f32[512]{0:T(512)S(1)} %add_rsqrt_fusion), kind=kOutput, calls=%fused_computation | convolution fusion | flops 8623489024 | bytes 26249216 | tf_op jit(solution)/shard_map/dot_general | solution.py:25
  112.1 0.0 copy-start.2
  112.1 0.0 reduce-scatter.5.cloned.1.call-update
  112.1 24.9 %all-gather.4.cloned.1.call-done = bf16[512,1024]{1,0:T(8,128)(2,1)} async-done(((bf16[512,128]{1,0:T(8,128)(2,1)}), bf16[512,1024]{1,0:T(8,128)(2,1)}) %all-gather.4.cloned.1.call-update) | async-done | bytes 1048592 | tf_op jit(solution)/shard_map/all_gather | solution.py:57
  137.1 0.0 copy-done.2
  137.1 2.6 fusion.23
  139.7 89.4 %all-gather.6.cloned.1.call-done = bf16[1,8192,1024]{2,1,0:T(8,128)(2,1)} async-done(((bf16[1,512,1024]{2,1,0:T(8,128)(2,1)}), bf16[1,8192,1024]{2,1,0:T(8,128)(2,1)}) %all-gather.6.cloned.1.call-update) | async-done | bytes 16777232 | tf_op jit(solution)/shard_map/all_gather | solution.py:19
  229.1 17.4 %fusion.4 = (f32[512]{0:T(512)S(1)}, f32[512,8192]{1,0:T(8,128)}) fusion(bf16[512,8192]{1,0:T(8,128)(2,1)} %param.9, f32[8192]{0:T(1024)S(1)} %copy-done.3, f32[512]{0:T(512)S(1)} %add_rsqrt_fusion, bf16[512,1024]{1,0:T(8,128)(2,1)S(1)} %copy-done, bf16[1,8192,1024]{2,1,0:T(8,128)(2,1)} %all-gather.6.cloned.1.call-done), kind=kOutput, calls=%fused_computation.7 | convolution fusion | flops 8610906112 | bytes 43028480 | tf_op jit(solution)/shard_map/dot_general | solution.py:22
  246.4 12.5 %fusion.7 = bf16[512,8192]{1,0:T(8,128)(2,1)} fusion(bf16[512,8192]{1,0:T(8,128)(2,1)} %param.9, f32[512,8192]{1,0:T(8,128)} %get-tuple-element.10, f32[512]{0:T(512)S(1)} %broadcast_multiply_fusion, f32[8192]{0:T(1024)S(1)} %copy-done.3, f32[512]{0:T(512)S(1)} %add_rsqrt_fusion), kind=kLoop, calls=%fused_computation.10 | loop fusion | flops 29360128 | bytes 33591296 | tf_op jit(solution)/shard_map/convert_element_type | solution.py:39
  258.9 15.9 %fusion.18 = bf16[512,1024]{1,0:T(8,128)(2,1)} fusion(bf16[1,8192,1024]{2,1,0:T(8,128)(2,1)} %all-gather.6.cloned.1.call-done, bf16[512,8192]{1,0:T(8,128)(2,1)} %param.9, f32[8192]{0:T(1024)S(1)} %copy-done.3, f32[512]{0:T(512)S(1)} %add_rsqrt_fusion), kind=kOutput, calls=%fused_computation.21 | convolution fusion | flops 8607236096 | bytes 26249216 | tf_op jit(solution)/shard_map/dot_general | solution.py:21
  274.9 134.3 %reduce-scatter.5.cloned.1.call-done = bf16[512,1024]{1,0:T(8,128)(2,1)} async-done(((bf16[8192,1024]{1,0:T(8,128)(2,1)}), bf16[512,1024]{1,0:T(8,128)(2,1)}) %reduce-scatter.5.cloned.1.call-update) | async-done | bytes 1048592 | tf_op jit(solution)/shard_map/reduce_scatter | solution.py:28
  409.1 0.0 copy-done.1
  (3 shorter events, 0.0 us)
Async XLA Ops:
  7.2 88.4 %copy-start = (bf16[512,1024]{1,0:T(8,128)(2,1)S(1)}, bf16[512,1024]{1,0:T(8,128)(2,1)}, u32[]{:S(2)}) copy-start(bf16[512,1024]{1,0:T(8,128)(2,1)} %param.12) | copy-start | bytes 3145732
  7.2 88.4 %copy-start.3 = (f32[8192]{0:T(1024)S(1)}, f32[8192]{0:T(1024)}, u32[]{:S(2)}) copy-start(f32[8192]{0:T(1024)} %param.10) | copy-start | bytes 98308
  7.2 79.5 %reduce-scatter.7.cloned.1.call-start = ((), (), s32[]{:S(2)}) async-start(), calls=%async_computation.5 | async-start | bytes 1179648
  11.9 125.2 %all-gather.4.cloned.1.call-start = ((), (), s32[]{:S(2)}) async-start(), calls=%async_computation.3 | async-start | bytes 1179648 | tf_op jit(solution)/shard_map/all_gather | solution.py:57
  89.7 139.4 %all-gather.6.cloned.1.call-start = ((), (), s32[]{:S(2)}) async-start(), calls=%async_computation.4 | async-start | bytes 17825792 | tf_op jit(solution)/shard_map/all_gather | solution.py:19
  90.4 318.7 %reduce-scatter.5.cloned.1.call-start = ((), (), s32[]{:S(2)}) async-start(), calls=%async_computation.2 | async-start | bytes 17825792 | tf_op jit(solution)/shard_map/reduce_scatter | solution.py:28
  112.1 25.0 %copy-start.2 = (bf16[1,512,1024]{2,1,0:T(8,128)(2,1)S(1)}, bf16[1,512,1024]{2,1,0:T(8,128)(2,1)}, u32[]{:S(2)}) copy-start(bf16[1,512,1024]{2,1,0:T(8,128)(2,1)} %param.15) | copy-start | bytes 3145732
  258.9 150.2 %copy-start.1 = (bf16[512,1024]{1,0:T(8,128)(2,1)S(1)}, bf16[512,1024]{1,0:T(8,128)(2,1)}, u32[]{:S(2)}) copy-start(bf16[512,1024]{1,0:T(8,128)(2,1)} %param.12) | copy-start | bytes 3145732
Sparse Core Ops, SparseCore 0:
  12.2 74.4 reduce-scatter.6
  89.8 47.2 all-gather.3
  138.9 90.1 all-gather.5
  232.0 177.0 reduce-scatter.4
where the time goes:
time: 422 us; the launch traced here: 416 us
  waiting for transfers between devices  324 us (77%)
  matrix products  49.8 us (12%)
  other arithmetic  24.7 us (6%)
  between operations  13.8 us (3%)
    reduce_scatter x1, waiting for transfers between devices, per_device(): lax.psum_scatter((term / groups).astype(jnp.bfloat16), 'fsdp', scatter_di...  134 us
    all_gather x1, waiting for transfers between devices, per_device(): piece = lax.all_gather(weight, 'fsdp', axis=0, tiled=True)  89.4 us
    unnamed x5, waiting for transfers between devices  75.5 us
    all_gather x1, waiting for transfers between devices, per_device(): lax.all_gather(new_global.astype(jnp.bfloat16), 'rep', axis=1, tiled=True)  24.9 us
    dot_general x1, matrix products, per_device(): lax.dot_general(cotangent, piece, contract, preferred_element_type=jnp.fl...  17.4 us
    dot_general x1, matrix products, per_device(): lax.dot_general(columns, cotangent, (((0,), (0,)), ((), ())), preferred_e...  16.5 us
    dot_general x1, matrix products, per_device(): outs = jnp.dot(columns, piece, preferred_element_type=jnp.float32)  15.9 us
    convert_element_type x1, other arithmetic, per_device(): token_gradient = (inverse_root_mean * (norm_gain - centered_tokens * jnp....  12.5 us
  transfers between devices with their start and end apart: 4, of which 4 were waited for; matrix products, arithmetic and copies ran while one was open for 17% of the time, Pallas kernels for 0%

commit v1 on v0

v1 whole, which is shorter than its diff:
```python
import jax
import jax.numpy as jnp
from jax import lax
from jax.experimental import pallas as pl
from jax.experimental.pallas import tpu as pltpu
from jax.sharding import PartitionSpec as P

F32 = jnp.float32
BF16 = jnp.bfloat16
NX, NZ, NC, NY, NH = 4, 2, 2, 4, 2
NEAR = ((0, 0), (1, 0), (3, 0), (0, 1))
FAR = ((2, 0), (1, 1), (3, 1), (2, 1))
VMEM = 40 * 2**20


def fsdp_index(x, z, c):
    return ((x % NX) * NZ + z % NZ) * NC + c % NC


def move(value, dx=0, dz=0, dc=0):
    pairs = [
        (fsdp_index(x, z, c), fsdp_index(x + dx, z + dz, c + dc))
        for x in range(NX)
        for z in range(NZ)
        for c in range(NC)
    ]
    return lax.ppermute(value, "fsdp", pairs)


def move_rep(value, dy=0, dh=0):
    pairs = [
        (y * NH + h, ((y + dy) % NY) * NH + (h + dh) % NH) for y in range(NY) for h in range(NH)
    ]
    return lax.ppermute(value, "rep", pairs)


def shard_order(places, dc):
    me = lax.axis_index("fsdp")
    x, z, c = me // (NZ * NC), (me // NC) % NZ, me % NC
    return jnp.stack([fsdp_index(x + dx, z + dz, c + dc) for dx, dz in places]).astype(jnp.int32)


def params():
    return pltpu.CompilerParams(
        vmem_limit_bytes=VMEM, dimension_semantics=("arbitrary",)
    )


def weight_term(tokens, gain, scaled_cot, order, other, groups):
    rows, width = tokens.shape
    outs = scaled_cot.shape[1]
    count = order.shape[0]
    depth = width // (NX * NZ * NC)

    def body(order_ref, tok_ref, gain_ref, cot_ref, *rest):
        out_ref = rest[-1]
        left = (tok_ref[...].astype(F32) * gain_ref[...]).astype(BF16)
        term = lax.dot_general(
            left, cot_ref[...], (((0,), (0,)), ((), ())), preferred_element_type=F32
        ) * (1.0 / groups)
        if len(rest) > 1:
            term = term + rest[0][0].astype(F32)
        out_ref[0] = term.astype(BF16)

    block = pl.BlockSpec((1, depth, outs), lambda k, o: (k, 0, 0))
    in_specs = [
        pl.BlockSpec((rows, depth), lambda k, o: (0, o[k])),
        pl.BlockSpec((1, depth), lambda k, o: (0, o[k])),
        pl.BlockSpec((rows, outs), lambda k, o: (0, 0)),
    ]
    args = [order, tokens, gain, scaled_cot]
    if other is not None:
        in_specs.append(block)
        args.append(other)
    return pl.pallas_call(
        body,
        out_shape=jax.ShapeDtypeStruct((count, depth, outs), BF16),
        grid_spec=pltpu.PrefetchScalarGridSpec(
            num_scalar_prefetch=1, grid=(count,), in_specs=in_specs, out_specs=block
        ),
        compiler_params=params(),
        cost_estimate=pl.CostEstimate(
            flops=2 * rows * depth * count * outs,
            bytes_accessed=count * depth * (rows + 2 * outs) * 2,
            transcendentals=0,
        ),
    )(*args)


def forward(tokens, gain, order, weights, total):
    rows, width = tokens.shape
    count, depth, outs = weights.shape

    def body(order_ref, tok_ref, gain_ref, w_ref, *rest):
        out_ref = rest[-1]
        left = (tok_ref[...].astype(F32) * gain_ref[...]).astype(BF16)
        term = jnp.dot(left, w_ref[0], preferred_element_type=F32)

        @pl.when(pl.program_id(0) == 0)
        def _():
            out_ref[...] = term + rest[0][...] if len(rest) > 1 else term

        @pl.when(pl.program_id(0) > 0)
        def _():
            out_ref[...] += term

    whole = pl.BlockSpec((rows, outs), lambda k, o: (0, 0))
    in_specs = [
        pl.BlockSpec((rows, depth), lambda k, o: (0, o[k])),
        pl.BlockSpec((1, depth), lambda k, o: (0, o[k])),
        pl.BlockSpec((1, depth, outs), lambda k, o: (k, 0, 0)),
    ]
    args = [order, tokens, gain, weights]
    if total is not None:
        in_specs.append(whole)
        args.append(total)
    return pl.pallas_call(
        body,
        out_shape=jax.ShapeDtypeStruct((rows, outs), F32),
        grid_spec=pltpu.PrefetchScalarGridSpec(
            num_scalar_prefetch=1, grid=(count,), in_specs=in_specs, out_specs=whole
        ),
        compiler_params=params(),
        cost_estimate=pl.CostEstimate(
            flops=2 * rows * depth * count * outs,
            bytes_accessed=count * depth * (rows + outs) * 2,
            transcendentals=0,
        ),
    )(*args)


def backward(tokens, gain, cotangent, rinv, mean, order, weights):
    rows, width = tokens.shape
    per, depth, outs = weights[0].shape
    sets = len(weights)

    def body(order_ref, tok_ref, gain_ref, cot_ref, rinv_ref, mean_ref, *rest):
        out_ref = rest[-1]
        step = pl.program_id(0)
        scale = rinv_ref[...]

        def one(w_ref):
            back = lax.dot_general(
                cot_ref[...], w_ref[0], (((1,), (1,)), ((), ())), preferred_element_type=F32
            )
            hat = tok_ref[...].astype(F32) * scale
            out_ref[...] = (scale * (back * gain_ref[...] - hat * mean_ref[...])).astype(BF16)

        for j in range(sets):
            pl.when(step // per == j)(lambda j=j: one(rest[j]))

    def weight_spec(j):
        return pl.BlockSpec(
            (1, depth, outs), lambda k, o: (jnp.clip(k - j * per, 0, per - 1), 0, 0)
        )

    column = pl.BlockSpec((rows, 1), lambda k, o: (0, 0))
    block = pl.BlockSpec((rows, depth), lambda k, o: (0, o[k]))
    return pl.pallas_call(
        body,
        out_shape=jax.ShapeDtypeStruct((rows, width), BF16),
        grid_spec=pltpu.PrefetchScalarGridSpec(
            num_scalar_prefetch=1,
            grid=(per * sets,),
            in_specs=[
                block,
                pl.BlockSpec((1, depth), lambda k, o: (0, o[k])),
                pl.BlockSpec((rows, outs), lambda k, o: (0, 0)),
                column,
                column,
            ]
            + [weight_spec(j) for j in range(sets)],
            out_specs=block,
        ),
        compiler_params=params(),
        cost_estimate=pl.CostEstimate(
            flops=2 * rows * width * outs,
            bytes_accessed=width * (2 * rows + outs) * 2,
            transcendentals=0,
        ),
    )(order, tokens, gain, cotangent, rinv, mean, *weights)


def gather_weight(own):
    depth = own.shape[0]
    half = depth // 2
    a, b = (depth // 3 + 15) // 16 * 16, depth - (depth // 3 + 15) // 16 * 16
    xm = move(own, dx=1)
    xp = move(own, dx=-1)
    zz = move(own, dz=1)
    near = jnp.stack([own, xp, xm, zz])
    near_other = move(near, dc=1)
    r1 = move(jnp.concatenate([zz[:half], xm[:half]]), dx=1)
    r2 = move(jnp.concatenate([zz[:half], xp[half:]]), dx=-1)
    r3 = move(jnp.concatenate([xp[half:], xm[half:]]), dz=1)
    x2 = jnp.concatenate([r1[half:], r2[half:]])
    zxp = jnp.concatenate([r2[:half], r3[:half]])
    zxm = jnp.concatenate([r1[:half], r3[half:]])
    r4 = move(zxm[:a], dx=1)
    r5 = move(zxp[b:], dx=-1)
    r6 = move(x2[a:b], dz=1)
    zx2 = jnp.concatenate([r4, r6, r5])
    far = jnp.stack([x2, zxp, zxm, zx2])
    far_other = move(far, dc=1)
    return near, near_other, far, far_other


def add(*terms):
    total = terms[0].astype(F32)
    for term in terms[1:]:
        total = total + term.astype(F32)
    return total.astype(BF16)


def scatter_grad(far, near):
    x2, zxp, zxm, zx2 = (far[i] for i in range(4))
    own, xp, xm, zz = (near[i] for i in range(4))
    depth = own.shape[0]
    half = depth // 2
    a, b = (depth // 3 + 15) // 16 * 16, depth - (depth // 3 + 15) // 16 * 16
    q4 = move(zx2[:a], dx=-1)
    q5 = move(zx2[b:], dx=1)
    q6 = move(zx2[a:b], dz=1)
    q1 = move(
        jnp.concatenate(
            [add(zxm[:a], q4), zxm[a:half], x2[:a], add(x2[a:half], q6[: half - a])]
        ),
        dx=-1,
    )
    q2 = move(
        jnp.concatenate([zxp[:half], add(x2[half:b], q6[half - a :]), x2[b:]]), dx=1
    )
    q3 = move(jnp.concatenate([zxp[half:b], add(zxp[b:], q5), zxm[half:]]), dz=1)
    sxp = move(jnp.concatenate([xp[:half], add(xp[half:], q2[half:], q3[:half])]), dx=1)
    sxm = move(
        jnp.concatenate([add(xm[:half], q1[half:]), add(xm[half:], q3[half:])]), dx=-1
    )
    szz = move(jnp.concatenate([add(zz[:half], q1[:half], q2[:half]), zz[half:]]), dz=1)
    return add(own, sxp, sxm, szz)


def outer_step(codes, scales, local_frag, momentum, global_frag):
    rows, width = codes.shape
    blocks = scales.shape[1]
    delta = (
        (
            codes.astype(F32).reshape(rows, blocks, width // blocks)
            * scales.astype(F32)[..., None]
        )
        .reshape(rows, width)
        .astype(BF16)
    )
    me = lax.axis_index("rep")
    y, h = me // NH, me % NH
    wide = width // NY
    piece = wide // NH
    def columns(value, k):
        return lax.dynamic_slice_in_dim(value, ((y + k) % NY) * wide, wide, axis=1)
    total = columns(delta, 0).astype(F32)
    for got in [move_rep(columns(delta, k), dy=k) for k in range(1, NY)]:
        total = total + got.astype(F32)
    mine = lax.dynamic_slice_in_dim(total, h * piece, piece, axis=1)
    theirs = lax.dynamic_slice_in_dim(total, (1 - h) * piece, piece, axis=1)
    average = (mine + move_rep(theirs.astype(BF16), dh=1).astype(F32)) / (NY * NH)
    new_momentum = 0.9 * momentum + average
    new_global = global_frag - 0.7 * (average + 0.9 * new_momentum)
    sent = new_global.astype(BF16)
    got = move_rep(sent, dh=1)
    pair = jnp.where(
        h == 0, jnp.concatenate([sent, got], axis=1), jnp.concatenate([got, sent], axis=1)
    )
    full = jnp.zeros((rows, width), BF16)
    for k in range(NY):
        part = pair if k == 0 else move_rep(pair, dy=-k)
        full = lax.dynamic_update_slice_in_dim(full, part, ((y + k) % NY) * wide, axis=1)
    merged = (0.5 * local_frag.astype(F32) + 0.5 * full.astype(F32)).astype(BF16)
    return merged, new_momentum, new_global


def per_device(
    tokens, gain, value_weight, cotangent, codes, scales, local_frag, momentum, global_frag
):
    groups = NX * NZ * NC
    width = tokens.shape[1]
    gain_row = gain[None]
    near, near_other, far, far_other = gather_weight(value_weight[0])
    merged, new_momentum, new_global = outer_step(
        codes[0], scales[0], local_frag[0], momentum, global_frag
    )
    token_input = tokens.astype(F32)
    rinv = 1.0 / jnp.sqrt(jnp.mean(token_input * token_input, axis=-1, keepdims=True) + 1e-05)
    scaled_cot = (cotangent.astype(F32) * rinv).astype(BF16)
    own_order = [shard_order(FAR, 0), shard_order(NEAR, 0)]
    other_order = [shard_order(FAR, 1), shard_order(NEAR, 1)]
    terms = []
    for mine, theirs in zip(own_order, other_order):
        sent = weight_term(tokens, gain_row, scaled_cot, theirs, None, groups)
        terms.append(
            weight_term(tokens, gain_row, scaled_cot, mine, move(sent, dc=1), groups)
        )
    weight_grad = scatter_grad(*terms)

    total = None
    for weights, order in (
        (near, own_order[1]),
        (near_other, other_order[1]),
        (far, own_order[0]),
        (far_other, other_order[0]),
    ):
        total = forward(tokens, gain_row, order, weights, total)
    outs = total * rinv
    mean = jnp.sum(outs * cotangent.astype(F32), axis=-1, keepdims=True) / width
    token_gradient = backward(
        tokens,
        gain_row,
        cotangent,
        rinv,
        mean,
        jnp.concatenate([own_order[1], other_order[1], own_order[0], other_order[0]]),
        (near, near_other, far, far_other),
    )
    return (
        outs.astype(BF16),
        token_gradient,
        weight_grad[None],
        merged[None],
        new_momentum,
        new_global,
    )


def solution(mesh):
    return jax.shard_map(
        per_device,
        mesh=mesh,
        in_specs=(
            P(("rep", "fsdp"), None),
            P(),
            P("rep", "fsdp", None),
            P(("rep", "fsdp"), None),
            P("rep", "fsdp", None),
            P("rep", "fsdp", None),
            P("rep", "fsdp", None),
            P("fsdp", "rep"),
            P("fsdp", "rep"),
        ),
        out_specs=(
            P(("rep", "fsdp"), None),
            P(("rep", "fsdp"), None),
            P("rep", "fsdp", None),
            P("rep", "fsdp", None),
            P("fsdp", "rep"),
            P("fsdp", "rep"),
        ),
        check_vma=False,
    )
```

time: 422 us -> 246 us (0.58); the launches traced: 416 us -> 245 us
  waiting for transfers between devices: 324 us -> 96.1 us
  Pallas kernels: 0 us -> 69.2 us
  matrix products: 49.8 us -> 0 us
  starting transfers between devices: 0.16 us -> 34.4 us
  between operations: 13.8 us -> 1.16 us
  local copies, waits for them, and re-layouts: 3.09 us -> 12 us
  other arithmetic: 24.7 us -> 31.9 us
    reduce_scatter x1 -> x0, waiting for transfers between devices: 134 us -> none  [per_device(): lax.psum_scatter((term / groups).astype(jnp.bfloat16), 'fsdp', scatter_di...]
    all_gather x2 -> x0, waiting for transfers between devices: 114 us -> none  [the longest x1 89.4 us: per_device(): piece = lax.all_gather(weight, 'fsdp', axis=0, tiled=True)]
    ppermute x0 -> x30, waiting for transfers between devices: none -> 96.1 us  [the longest x22 70.9 us: move(): return lax.ppermute(value, 'fsdp', pairs)]
    unnamed x5 -> x0, waiting for transfers between devices: 75.5 us -> none
    pallas_call x0 -> x9, Pallas kernels: none -> 69.2 us  [the longest x4 25.3 us: forward(): pl.pallas_call(body, out_shape=jax.ShapeDtypeStruct((rows, outs), F32), g...]
    dot_general x3 -> x0, matrix products: 49.8 us -> none  [the longest x1 17.4 us: per_device(): lax.dot_general(cotangent, piece, contract, preferred_element_type=jnp.fl...]
    ppermute x0 -> x30, starting transfers between devices: none -> 34.4 us  [the longest x22 20.5 us: move(): return lax.ppermute(value, 'fsdp', pairs)]
    convert_element_type x4 -> x6, other arithmetic: 17 us -> 6.1 us  [the longest x3 3.38 us: add(): return total.astype(BF16)]
  transfers between devices with their start and end apart: 4 -> 30, of which waited for: 4 -> 16; matrix products, arithmetic and copies ran while one was open for 17% -> 11% of each run, Pallas kernels for 0% -> 24%
where the time goes in v1:
time: 246 us; the launch traced here: 245 us
  waiting for transfers between devices  96.1 us (39%)
  Pallas kernels  69.2 us (28%)
  starting transfers between devices  34.4 us (14%)
  other arithmetic  31.9 us (13%)
  local copies, waits for them, and re-layouts  12 us (5%)
    ppermute x22, waiting for transfers between devices, move(): return lax.ppermute(value, 'fsdp', pairs)  70.9 us
    pallas_call x4, Pallas kernels, forward(): pl.pallas_call(body, out_shape=jax.ShapeDtypeStruct((rows, outs), F32), g...  25.3 us
    ppermute x8, waiting for transfers between devices, move_rep(): return lax.ppermute(value, 'rep', pairs)  25.2 us
    pallas_call x1, Pallas kernels, backward(): pl.pallas_call(body, out_shape=jax.ShapeDtypeStruct((rows, width), BF16),...  22.4 us
    pallas_call x4, Pallas kernels, weight_term(): pl.pallas_call(body, out_shape=jax.ShapeDtypeStruct((count, depth, outs),...  21.5 us
    ppermute x22, starting transfers between devices, move(): return lax.ppermute(value, 'fsdp', pairs)  20.5 us
    ppermute x8, starting transfers between devices, move_rep(): return lax.ppermute(value, 'rep', pairs)  13.9 us
    unnamed x26, local copies, waits for them, and re-layouts  6.23 us
  transfers between devices with their start and end apart: 30, of which 16 were waited for; matrix products, arithmetic and copies ran while one was open for 11% of the time, Pallas kernels for 24%

profile of v1, /device:TPU:6, one launch (start us, length us, event | category | flops | bytes accessed | tf_op | source)
XLA Modules:
  0.0 244.8 jit_solution(7547048439352652449)
XLA Ops:
  5.9 20.1 %collective-permute-done = bf16[512,1024]{1,0:T(8,128)(2,1)S(1)} collective-permute-done((bf16[512,1024]{1,0:T(8,128)(2,1)}, bf16[512,1024]{1,0:T(8,128)(2,1)S(1)}, u32[]{:S(2)}, u32[]{:S(2)}) %collective-permute-start) | collective-permute-done | bytes 1048608 | tf_op jit(solution)/shard_map/ppermute | solution.py:27
  29.6 2.9 %collective-permute-start.2 = (bf16[512,1024]{1,0:T(8,128)(2,1)S(1)}, bf16[512,1024]{1,0:T(8,128)(2,1)S(1)}, u32[]{:S(2)}, u32[]{:S(2)}) collective-permute-start(bf16[512,1024]{1,0:T(8,128)(2,1)S(1)} %get-tuple-element.45), channel_id=1, source_target_pairs={{0,4},{1,5},{2,6},{3,7},{4,8},{5,9},{6,10},{7,11},{8,12},{9,13},{1... | collective-permute-start | bytes 3145736 | tf_op jit(solution)/shard_map/ppermute | solution.py:27
  34.9 18.1 %collective-permute-done.5 = bf16[512,1024]{1,0:T(8,128)(2,1)S(1)} collective-permute-done((bf16[512,1024]{1,0:T(8,128)(2,1)S(1)}, bf16[512,1024]{1,0:T(8,128)(2,1)S(1)}, u32[]{:S(2)}, u32[]{:S(2)}) %collective-permute-start.5) | collective-permute-done | bytes 1048608 | tf_op jit(solution)/shard_map/ppermute | solution.py:27
  53.5 5.5 %collective-permute-done.4 = bf16[512,1024]{1,0:T(8,128)(2,1)S(1)} collective-permute-done((bf16[512,1024]{1,0:T(8,128)(2,1)S(1)}, bf16[512,1024]{1,0:T(8,128)(2,1)S(1)}, u32[]{:S(2)}, u32[]{:S(2)}) %collective-permute-start.4) | collective-permute-done | bytes 1048608 | tf_op jit(solution)/shard_map/ppermute | solution.py:27
  61.6 4.8 %collective-permute-done.7 = bf16[160,1024]{1,0:T(8,128)(2,1)S(1)} collective-permute-done((bf16[160,1024]{1,0:T(8,128)(2,1)S(1)}, bf16[160,1024]{1,0:T(8,128)(2,1)S(1)}, u32[]{:S(2)}, u32[]{:S(2)}) %collective-permute-start.7) | collective-permute-done | bytes 327712 | tf_op jit(solution)/shard_map/ppermute | solution.py:27
  71.3 5.1 %multiply_reduce_fusion = f32[512]{0:T(512)S(1)} fusion(bf16[512,8192]{1,0:T(8,128)(2,1)} %tok_ref.17), kind=kLoop, calls=%fused_computation | loop fusion | flops 12582400 | bytes 8390656 | tf_op jit(solution)/shard_map/reduce_sum | solution.py:291
  76.4 6.2 %shard_map.136.rest_0_ = f32[512,1024]{1,0:T(8,128)S(1)} custom-call(s32[4]{0:T(128)S(1)} %pad_add_fusion.3.order_ref, bf16[512,8192]{1,0:T(8,128)(2,1)} %tok_ref.17, f32[1,8192]{1,0:T(1,128)S(1)} %bitcast.118, bf16[4,512,1024]{2,1,0:T(8,128)(2,1)} %pad_maximum_fusion.1.w_ref.rest_0_), custom_call_target="tpu_custom_call" | custom-call | flops 2147483648 | bytes 6291456 | tf_op jit(solution)/shard_map/pallas_call | solution.py:117
  82.6 6.2 %shard_map.137.rest_0_ = f32[512,1024]{1,0:T(8,128)S(1)} custom-call(s32[4]{0:T(128)S(1)} %pad_add_fusion.2.order_ref, bf16[512,8192]{1,0:T(8,128)(2,1)} %tok_ref.17, f32[1,8192]{1,0:T(1,128)S(1)} %bitcast.119, bf16[4,512,1024]{2,1,0:T(8,128)(2,1)} %collective-permute-done.10.w_ref.rest_1_, f32[512,1024]{1,0:T(8,128)S(1)} %shard_map.136.rest_0_), custom_call_target="tpu_custom_call" | custom-call | flops 2147483648 | bytes 6291456 | tf_op jit(solution)/shard_map/pallas_call | solution.py:117
  88.9 6.5 %shard_map.138.rest_0_ = f32[512,1024]{1,0:T(8,128)S(1)} custom-call(s32[4]{0:T(128)S(1)} %pad_add_fusion.1.order_ref, bf16[512,8192]{1,0:T(8,128)(2,1)} %tok_ref.17, f32[1,8192]{1,0:T(1,128)S(1)} %bitcast.120, bf16[4,512,1024]{2,1,0:T(8,128)(2,1)} %pad_maximum_fusion.w_ref.rest_2_, f32[512,1024]{1,0:T(8,128)S(1)} %shard_map.137.rest_0_), custom_call_target="tpu_custom_call" | custom-call | flops 2147483648 | bytes 6291456 | tf_op jit(solution)/shard_map/pallas_call | solution.py:117
  95.4 6.4 %shard_map.139 = f32[512,1024]{1,0:T(8,128)S(1)} custom-call(s32[4]{0:T(128)S(1)} %pad_add_fusion.order_ref, bf16[512,8192]{1,0:T(8,128)(2,1)} %tok_ref.17, f32[1,8192]{1,0:T(1,128)S(1)} %bitcast.121, bf16[4,512,1024]{2,1,0:T(8,128)(2,1)} %collective-permute-done.9.w_ref.rest_3_, f32[512,1024]{1,0:T(8,128)S(1)} %shard_map.138.rest_0_), custom_call_target="tpu_custom_call" | custom-call | flops 2147483648 | bytes 6291456 | tf_op jit(solution)/shard_map/pallas_call | solution.py:117
  103.3 5.0 %shard_map.143 = bf16[4,512,1024]{2,1,0:T(8,128)(2,1)} custom-call(s32[4]{0:T(128)S(1)} %pad_add_fusion.order_ref, bf16[512,8192]{1,0:T(8,128)(2,1)S(1)} %bitcast.117, f32[1,8192]{1,0:T(1,128)S(1)} %bitcast.122, bf16[512,1024]{1,0:T(8,128)(2,1)S(1)} %get-tuple-element.31.cot_ref), custom_call_target="tpu_custom_call" | custom-call | flops 2147483648 | bytes 10485760 | tf_op jit(solution)/shard_map/pallas_call | solution.py:75
  109.0 3.4 %copy-done = bf16[512,8192]{1,0:T(8,128)(2,1)S(1)} copy-done((bf16[512,8192]{1,0:T(8,128)(2,1)S(1)}, bf16[512,8192]{1,0:T(8,128)(2,1)}, u32[]{:S(2)}) %copy-start) | copy-done | bytes 8388632
  112.3 4.9 %shard_map.141 = bf16[4,512,1024]{2,1,0:T(8,128)(2,1)} custom-call(s32[4]{0:T(128)S(1)} %pad_add_fusion.2.order_ref, bf16[512,8192]{1,0:T(8,128)(2,1)S(1)} %copy-done, f32[1,8192]{1,0:T(1,128)S(1)} %bitcast.123, bf16[512,1024]{1,0:T(8,128)(2,1)S(1)} %get-tuple-element.31.cot_ref), custom_call_target="tpu_custom_call" | custom-call | flops 2147483648 | bytes 10485760 | tf_op jit(solution)/shard_map/pallas_call | solution.py:75
  120.2 3.0 %collective-permute-start.24 = (bf16[512,256]{1,0:T(8,128)(2,1)}, bf16[512,256]{1,0:T(8,128)(2,1)}, u32[]{:S(2)}, u32[]{:S(2)}) collective-permute-start(bf16[512,256]{1,0:T(8,128)(2,1)} %get-tuple-element.33), channel_id=1, source_target_pairs={{0,96},{16,112},{32,0},{48,16},{64,32},{80,48},{96,64},{112,80},{1... | collective-permute-start | bytes 786440 | tf_op jit(solution)/shard_map/ppermute | solution.py:34
  124.8 10.1 %collective-permute-done.24 = bf16[512,256]{1,0:T(8,128)(2,1)} collective-permute-done((bf16[512,256]{1,0:T(8,128)(2,1)}, bf16[512,256]{1,0:T(8,128)(2,1)}, u32[]{:S(2)}, u32[]{:S(2)}) %collective-permute-start.24) | collective-permute-done | bytes 262176 | tf_op jit(solution)/shard_map/ppermute | solution.py:34
  134.9 3.5 %collective-permute-done.22 = bf16[512,256]{1,0:T(8,128)(2,1)} collective-permute-done((bf16[512,256]{1,0:T(8,128)(2,1)S(1)}, bf16[512,256]{1,0:T(8,128)(2,1)}, u32[]{:S(2)}, u32[]{:S(2)}) %collective-permute-start.22) | collective-permute-done | bytes 262176 | tf_op jit(solution)/shard_map/ppermute | solution.py:34
  140.5 4.2 %collective-permute-start.25 = (bf16[512,128]{1,0:T(8,128)(2,1)S(1)}, bf16[512,128]{1,0:T(8,128)(2,1)S(1)}, u32[]{:S(2)}, u32[]{:S(2)}) collective-permute-start(bf16[512,128]{1,0:T(8,128)(2,1)S(1)} %dynamic-slice_convert_fusion), channel_id=1, source_target_pairs={{0,16},{16,0},{32,48},{48,32},{64,80},{80,64},{96,112},{112,96},{1... | collective-permute-start | bytes 393224 | tf_op jit(solution)/shard_map/ppermute | solution.py:34
  144.7 3.5 %collective-permute-done.25 = bf16[512,128]{1,0:T(8,128)(2,1)S(1)} collective-permute-done((bf16[512,128]{1,0:T(8,128)(2,1)S(1)}, bf16[512,128]{1,0:T(8,128)(2,1)S(1)}, u32[]{:S(2)}, u32[]{:S(2)}) %collective-permute-start.25) | collective-permute-done | bytes 131104 | tf_op jit(solution)/shard_map/ppermute | solution.py:34
  150.3 3.2 %collective-permute-start.26 = (bf16[512,128]{1,0:T(8,128)(2,1)S(1)}, bf16[512,128]{1,0:T(8,128)(2,1)S(1)}, u32[]{:S(2)}, u32[]{:S(2)}) collective-permute-start(bf16[512,128]{1,0:T(8,128)(2,1)S(1)} %get-tuple-element.8), channel_id=1, source_target_pairs={{0,16},{16,0},{32,48},{48,32},{64,80},{80,64},{96,112},{112,96},{1... | collective-permute-start | bytes 393224 | tf_op jit(solution)/shard_map/ppermute | solution.py:34
  153.5 3.2 %collective-permute-done.26 = bf16[512,128]{1,0:T(8,128)(2,1)S(1)} collective-permute-done((bf16[512,128]{1,0:T(8,128)(2,1)S(1)}, bf16[512,128]{1,0:T(8,128)(2,1)S(1)}, u32[]{:S(2)}, u32[]{:S(2)}) %collective-permute-start.26) | collective-permute-done | bytes 131104 | tf_op jit(solution)/shard_map/ppermute | solution.py:34
  158.6 5.8 %shard_map.144 = bf16[4,512,1024]{2,1,0:T(8,128)(2,1)S(1)} custom-call(s32[4]{0:T(128)S(1)} %pad_add_fusion.1.order_ref, bf16[512,8192]{1,0:T(8,128)(2,1)} %tok_ref.17, f32[1,8192]{1,0:T(1,128)S(1)} %bitcast.124, bf16[512,1024]{1,0:T(8,128)(2,1)S(1)} %get-tuple-element.31.cot_ref, bf16[4,512,1024]{2,1,0:T(8,128)(2,1)} %collective-permute-done.12.rest_0_), custom_call_target="tpu_custom_call" | custom-call | flops 2147483648 | bytes 10485760 | tf_op jit(solution)/shard_map/pallas_call | solution.py:75
  166.1 6.1 %collective-permute-done.13 = bf16[160,1024]{1,0:T(8,128)(2,1)S(1)} collective-permute-done((bf16[160,1024]{1,0:T(8,128)(2,1)S(1)}, bf16[160,1024]{1,0:T(8,128)(2,1)S(1)}, u32[]{:S(2)}, u32[]{:S(2)}) %collective-permute-start.13) | collective-permute-done | bytes 327712 | tf_op jit(solution)/shard_map/ppermute | solution.py:27
  173.3 3.2 %collective-permute-start.14 = (bf16[512,1024]{1,0:T(8,128)(2,1)}, bf16[512,1024]{1,0:T(8,128)(2,1)}, u32[]{:S(2)}, u32[]{:S(2)}) collective-permute-start(bf16[512,1024]{1,0:T(8,128)(2,1)} %pad_maximum_fusion.6), channel_id=1, source_target_pairs={{0,4},{1,5},{2,6},{3,7},{4,8},{5,9},{6,10},{7,11},{8,12},{9,13},{1... | collective-permute-start | bytes 3145736 | tf_op jit(solution)/shard_map/ppermute | solution.py:27
  176.6 4.3 %collective-permute-done.18 = bf16[176,1024]{1,0:T(8,128)(2,1)S(1)} collective-permute-done((bf16[176,1024]{1,0:T(8,128)(2,1)S(1)}, bf16[176,1024]{1,0:T(8,128)(2,1)S(1)}, u32[]{:S(2)}, u32[]{:S(2)}) %collective-permute-start.18) | collective-permute-done | bytes 360480 | tf_op jit(solution)/shard_map/ppermute | solution.py:27
  188.3 4.8 %collective-permute-done.29 = bf16[512,256]{1,0:T(8,128)(2,1)} collective-permute-done((bf16[512,256]{1,0:T(8,128)(2,1)}, bf16[512,256]{1,0:T(8,128)(2,1)}, u32[]{:S(2)}, u32[]{:S(2)}) %collective-permute-start.29) | collective-permute-done | bytes 262176 | tf_op jit(solution)/shard_map/ppermute | solution.py:34
  194.2 5.8 %shard_map.142 = bf16[4,512,1024]{2,1,0:T(8,128)(2,1)S(1)} custom-call(s32[4]{0:T(128)S(1)} %pad_add_fusion.3.order_ref, bf16[512,8192]{1,0:T(8,128)(2,1)} %tok_ref.17, f32[1,8192]{1,0:T(1,128)S(1)} %bitcast.125, bf16[512,1024]{1,0:T(8,128)(2,1)S(1)} %get-tuple-element.31.cot_ref, bf16[4,512,1024]{2,1,0:T(8,128)(2,1)} %collective-permute-done.11.rest_0_), custom_call_target="tpu_custom_call" | custom-call | flops 2147483648 | bytes 10485760 | tf_op jit(solution)/shard_map/pallas_call | solution.py:75
  200.1 3.4 %collective-permute-done.16 = bf16[512,1024]{1,0:T(8,128)(2,1)} collective-permute-done((bf16[512,1024]{1,0:T(8,128)(2,1)}, bf16[512,1024]{1,0:T(8,128)(2,1)}, u32[]{:S(2)}, u32[]{:S(2)}) %collective-permute-start.16) | collective-permute-done | bytes 1048608 | tf_op jit(solution)/shard_map/ppermute | solution.py:27
  203.5 3.2 %collective-permute-done.19 = bf16[512,1024]{1,0:T(8,128)(2,1)} collective-permute-done((bf16[512,1024]{1,0:T(8,128)(2,1)}, bf16[512,1024]{1,0:T(8,128)(2,1)}, u32[]{:S(2)}, u32[]{:S(2)}) %collective-permute-start.19) | collective-permute-done | bytes 1048608 | tf_op jit(solution)/shard_map/ppermute | solution.py:27
  206.7 3.0 %fusion.16 = (bf16[256,1024]{1,0:T(8,128)(2,1)S(1)}, bf16[256,1024]{1,0:T(8,128)(2,1)S(1)}, bf16[256,1024]{1,0:T(8,128)(2,1)S(1)}, bf16[256,1024]{1,0:T(8,128)(2,1)S(1)}) fusion(bf16[512,1024]{1,0:T(8,128)(2,1)} %collective-permute-done.16, bf16[512,1024]{1,0:T(8,128)(2,1)} %collective-permute-done.14, bf16[4,512,1024]{2,1,0:T(8,128)(2,1)S(1)} %shard_map.142, ...), kind=kLoop, calls=%fused_computation.45 | loop fusion | flops 5242880 | bytes 7340032 | tf_op jit(solution)/shard_map/convert_element_type | solution.py:212
  213.9 3.2 %collective-permute-start.17 = (bf16[512,1024]{1,0:T(8,128)(2,1)}, bf16[512,1024]{1,0:T(8,128)(2,1)S(1)}, u32[]{:S(2)}, u32[]{:S(2)}) collective-permute-start(bf16[512,1024]{1,0:T(8,128)(2,1)} %pad_maximum_fusion.8), channel_id=1, source_target_pairs={{0,4},{1,5},{2,6},{3,7},{4,8},{5,9},{6,10},{7,11},{8,12},{9,13},{1... | collective-permute-start | bytes 3145736 | tf_op jit(solution)/shard_map/ppermute | solution.py:27
  218.6 22.4 %shard_map.140 = bf16[512,8192]{1,0:T(8,128)(2,1)} custom-call(s32[16]{0:T(128)S(1)} %concatenate.56.order_ref, bf16[512,8192]{1,0:T(8,128)(2,1)} %tok_ref.17, f32[1,8192]{1,0:T(1,128)S(1)} %bitcast.126, bf16[512,1024]{1,0:T(8,128)(2,1)S(1)} %copy-done.2, f32[512,1]{1,0:T(8,128)S(1)} %copy.16.rinv_ref, f32[512,1]{1,0:T(8,128)S(1)} %copy.17.mean_ref, ...), custom_call_target="tpu_custom_call" | custom-call | flops 8589934592 | bytes 33554432 | tf_op jit(solution)/shard_map/pallas_call | solution.py:159
  241.0 3.7 %fusion.9 = bf16[1,512,1024]{2,1,0:T(8,128)(2,1)} fusion(bf16[512,1024]{1,0:T(8,128)(2,1)} %collective-permute-done.21, bf16[512,1024]{1,0:T(8,128)(2,1)} %collective-permute-done.20, bf16[512,1024]{1,0:T(8,128)(2,1)S(1)} %collective-permute-done.17, bf16[4,512,1024]{2,1,0:T(8,128)(2,1)} %copy-done.1), kind=kLoop, calls=%fused_computation.23 | loop fusion | flops 4194304 | bytes 5242880 | tf_op jit(solution)/shard_map/broadcast_in_dim | solution.py:325
  (119 shorter events, 48.5 us)
Async XLA Ops:
  0.6 25.4 %collective-permute-start = (bf16[512,1024]{1,0:T(8,128)(2,1)}, bf16[512,1024]{1,0:T(8,128)(2,1)S(1)}, u32[]{:S(2)}, u32[]{:S(2)}) collective-permute-start(bf16[512,1024]{1,0:T(8,128)(2,1)} %bitcast.131), channel_id=1, source_target_pairs={{0,2},{1,3},{2,0},{3,1},{4,6},{5,7},{6,4},{7,5},{8,10},{9,11},{10,... | collective-permute-start | bytes 3145736 | tf_op jit(solution)/shard_map/ppermute | solution.py:27
  2.6 26.0 %collective-permute-start.3 = (bf16[512,1024]{1,0:T(8,128)(2,1)}, bf16[512,1024]{1,0:T(8,128)(2,1)S(1)}, u32[]{:S(2)}, u32[]{:S(2)}) collective-permute-start(bf16[512,1024]{1,0:T(8,128)(2,1)} %bitcast.132), channel_id=1, source_target_pairs={{0,12},{1,13},{2,14},{3,15},{4,0},{5,1},{6,2},{7,3},{8,4},{9,5},{1... | collective-permute-start | bytes 3145736 | tf_op jit(solution)/shard_map/ppermute | solution.py:27
  3.5 25.3 %collective-permute-start.1 = (bf16[512,1024]{1,0:T(8,128)(2,1)}, bf16[512,1024]{1,0:T(8,128)(2,1)S(1)}, u32[]{:S(2)}, u32[]{:S(2)}) collective-permute-start(bf16[512,1024]{1,0:T(8,128)(2,1)} %bitcast.133), channel_id=1, source_target_pairs={{0,4},{1,5},{2,6},{3,7},{4,8},{5,9},{6,10},{7,11},{8,12},{9,13},{1... | collective-permute-start | bytes 3145736 | tf_op jit(solution)/shard_map/ppermute | solution.py:27
  29.2 23.8 %collective-permute-start.5 = (bf16[512,1024]{1,0:T(8,128)(2,1)S(1)}, bf16[512,1024]{1,0:T(8,128)(2,1)S(1)}, u32[]{:S(2)}, u32[]{:S(2)}) collective-permute-start(bf16[512,1024]{1,0:T(8,128)(2,1)S(1)} %get-tuple-element.44), channel_id=1, source_target_pairs={{0,2},{1,3},{2,0},{3,1},{4,6},{5,7},{6,4},{7,5},{8,10},{9,11},{10,... | collective-permute-start | bytes 3145736 | tf_op jit(solution)/shard_map/ppermute | solution.py:27
  29.6 23.8 %collective-permute-start.2 = (bf16[512,1024]{1,0:T(8,128)(2,1)S(1)}, bf16[512,1024]{1,0:T(8,128)(2,1)S(1)}, u32[]{:S(2)}, u32[]{:S(2)}) collective-permute-start(bf16[512,1024]{1,0:T(8,128)(2,1)S(1)} %get-tuple-element.45), channel_id=1, source_target_pairs={{0,4},{1,5},{2,6},{3,7},{4,8},{5,9},{6,10},{7,11},{8,12},{9,13},{1... | collective-permute-start | bytes 3145736 | tf_op jit(solution)/shard_map/ppermute | solution.py:27
  32.5 26.5 %collective-permute-start.4 = (bf16[512,1024]{1,0:T(8,128)(2,1)S(1)}, bf16[512,1024]{1,0:T(8,128)(2,1)S(1)}, u32[]{:S(2)}, u32[]{:S(2)}) collective-permute-start(bf16[512,1024]{1,0:T(8,128)(2,1)S(1)} %get-tuple-element.43), channel_id=1, source_target_pairs={{0,12},{1,13},{2,14},{3,15},{4,0},{5,1},{6,2},{7,3},{8,4},{9,5},{1... | collective-permute-start | bytes 3145736 | tf_op jit(solution)/shard_map/ppermute | solution.py:27
  34.9 47.7 %collective-permute-start.10 = (bf16[4,512,1024]{2,1,0:T(8,128)(2,1)}, bf16[4,512,1024]{2,1,0:T(8,128)(2,1)}, u32[]{:S(2)}, u32[]{:S(2)}) collective-permute-start(bf16[4,512,1024]{2,1,0:T(8,128)(2,1)} %pad_maximum_fusion.1.w_ref.rest_0_), channel_id=1, source_target_pairs={{0,1},{1,0},{2,3},{3,2},{4,5},{5,4},{6,7},{7,6},{8,9},{9,8},{10,11... | collective-permute-start | bytes 12582920 | tf_op jit(solution)/shard_map/ppermute | solution.py:27
  53.0 13.3 %collective-permute-start.8 = (bf16[176,1024]{1,0:T(8,128)(2,1)S(1)}, bf16[176,1024]{1,0:T(8,128)(2,1)S(1)}, u32[]{:S(2)}, u32[]{:S(2)}) collective-permute-start(bf16[176,1024]{1,0:T(8,128)(2,1)S(1)} %slice.259), channel_id=1, source_target_pairs={{0,12},{1,13},{2,14},{3,15},{4,0},{5,1},{6,2},{7,3},{8,4},{9,5},{1... | collective-permute-start | bytes 1081352 | tf_op jit(solution)/shard_map/ppermute | solution.py:27
  59.2 7.2 %collective-permute-start.7 = (bf16[160,1024]{1,0:T(8,128)(2,1)S(1)}, bf16[160,1024]{1,0:T(8,128)(2,1)S(1)}, u32[]{:S(2)}, u32[]{:S(2)}) collective-permute-start(bf16[160,1024]{1,0:T(8,128)(2,1)S(1)} %fusion.19), channel_id=1, source_target_pairs={{0,2},{1,3},{2,0},{3,1},{4,6},{5,7},{6,4},{7,5},{8,10},{9,11},{10,... | collective-permute-start | bytes 983048 | tf_op jit(solution)/shard_map/ppermute | solution.py:27
  61.1 7.5 %collective-permute-start.6 = (bf16[176,1024]{1,0:T(8,128)(2,1)S(1)}, bf16[176,1024]{1,0:T(8,128)(2,1)S(1)}, u32[]{:S(2)}, u32[]{:S(2)}) collective-permute-start(bf16[176,1024]{1,0:T(8,128)(2,1)S(1)} %slice.256), channel_id=1, source_target_pairs={{0,4},{1,5},{2,6},{3,7},{4,8},{5,9},{6,10},{7,11},{8,12},{9,13},{1... | collective-permute-start | bytes 1081352 | tf_op jit(solution)/shard_map/ppermute | solution.py:27
  71.0 24.4 %collective-permute-start.9 = (bf16[4,512,1024]{2,1,0:T(8,128)(2,1)}, bf16[4,512,1024]{2,1,0:T(8,128)(2,1)}, u32[]{:S(2)}, u32[]{:S(2)}) collective-permute-start(bf16[4,512,1024]{2,1,0:T(8,128)(2,1)} %pad_maximum_fusion.w_ref.rest_2_), channel_id=1, source_target_pairs={{0,1},{1,0},{2,3},{3,2},{4,5},{5,4},{6,7},{7,6},{8,9},{9,8},{10,11... | collective-permute-start | bytes 12582920 | tf_op jit(solution)/shard_map/ppermute | solution.py:27
  88.9 14.4 %slice-start = ((s8[8388608]{0:T(1024)(128)(4,1)}), s8[4194304]{0:T(1024)(128)(4,1)S(1)}, s32[]{:S(2)}) async-start(s8[8388608]{0:T(1024)(128)(4,1)} %bitcast.116), calls=%async_computation | async-start | bytes 8388608
  108.3 50.3 %collective-permute-start.12 = (bf16[4,512,1024]{2,1,0:T(8,128)(2,1)}, bf16[4,512,1024]{2,1,0:T(8,128)(2,1)}, u32[]{:S(2)}, u32[]{:S(2)}) collective-permute-start(bf16[4,512,1024]{2,1,0:T(8,128)(2,1)} %shard_map.143), channel_id=1, source_target_pairs={{0,1},{1,0},{2,3},{3,2},{4,5},{5,4},{6,7},{7,6},{8,9},{9,8},{10,11... | collective-permute-start | bytes 12582920 | tf_op jit(solution)/shard_map/ppermute | solution.py:27
  117.3 76.9 %collective-permute-start.11 = (bf16[4,512,1024]{2,1,0:T(8,128)(2,1)}, bf16[4,512,1024]{2,1,0:T(8,128)(2,1)}, u32[]{:S(2)}, u32[]{:S(2)}) collective-permute-start(bf16[4,512,1024]{2,1,0:T(8,128)(2,1)} %shard_map.141), channel_id=1, source_target_pairs={{0,1},{1,0},{2,3},{3,2},{4,5},{5,4},{6,7},{7,6},{8,9},{9,8},{10,11... | collective-permute-start | bytes 12582920 | tf_op jit(solution)/shard_map/ppermute | solution.py:27
  120.2 14.7 %collective-permute-start.24 = (bf16[512,256]{1,0:T(8,128)(2,1)}, bf16[512,256]{1,0:T(8,128)(2,1)}, u32[]{:S(2)}, u32[]{:S(2)}) collective-permute-start(bf16[512,256]{1,0:T(8,128)(2,1)} %get-tuple-element.33), channel_id=1, source_target_pairs={{0,96},{16,112},{32,0},{48,16},{64,32},{80,48},{96,64},{112,80},{1... | collective-permute-start | bytes 786440 | tf_op jit(solution)/shard_map/ppermute | solution.py:34
  123.2 11.7 %collective-permute-start.23 = (bf16[512,256]{1,0:T(8,128)(2,1)}, bf16[512,256]{1,0:T(8,128)(2,1)}, u32[]{:S(2)}, u32[]{:S(2)}) collective-permute-start(bf16[512,256]{1,0:T(8,128)(2,1)} %get-tuple-element.34), channel_id=1, source_target_pairs={{0,64},{16,80},{32,96},{48,112},{64,0},{80,16},{96,32},{112,48},{1... | collective-permute-start | bytes 786440 | tf_op jit(solution)/shard_map/ppermute | solution.py:34
  123.8 14.6 %collective-permute-start.22 = (bf16[512,256]{1,0:T(8,128)(2,1)S(1)}, bf16[512,256]{1,0:T(8,128)(2,1)}, u32[]{:S(2)}, u32[]{:S(2)}) collective-permute-start(bf16[512,256]{1,0:T(8,128)(2,1)S(1)} %get-tuple-element.32), channel_id=1, source_target_pairs={{0,32},{16,48},{32,64},{48,80},{64,96},{80,112},{96,0},{112,16},{1... | collective-permute-start | bytes 786440 | tf_op jit(solution)/shard_map/ppermute | solution.py:34
  140.5 7.8 %collective-permute-start.25 = (bf16[512,128]{1,0:T(8,128)(2,1)S(1)}, bf16[512,128]{1,0:T(8,128)(2,1)S(1)}, u32[]{:S(2)}, u32[]{:S(2)}) collective-permute-start(bf16[512,128]{1,0:T(8,128)(2,1)S(1)} %dynamic-slice_convert_fusion), channel_id=1, source_target_pairs={{0,16},{16,0},{32,48},{48,32},{64,80},{80,64},{96,112},{112,96},{1... | collective-permute-start | bytes 393224 | tf_op jit(solution)/shard_map/ppermute | solution.py:34
  150.3 6.5 %collective-permute-start.26 = (bf16[512,128]{1,0:T(8,128)(2,1)S(1)}, bf16[512,128]{1,0:T(8,128)(2,1)S(1)}, u32[]{:S(2)}, u32[]{:S(2)}) collective-permute-start(bf16[512,128]{1,0:T(8,128)(2,1)S(1)} %get-tuple-element.8), channel_id=1, source_target_pairs={{0,16},{16,0},{32,48},{48,32},{64,80},{80,64},{96,112},{112,96},{1... | collective-permute-start | bytes 393224 | tf_op jit(solution)/shard_map/ppermute | solution.py:34
  157.7 26.2 %collective-permute-start.27 = (bf16[512,256]{1,0:T(8,128)(2,1)}, bf16[512,256]{1,0:T(8,128)(2,1)S(1)}, u32[]{:S(2)}, u32[]{:S(2)}) collective-permute-start(bf16[512,256]{1,0:T(8,128)(2,1)} %get-tuple-element.7), channel_id=1, source_target_pairs={{0,96},{16,112},{32,0},{48,16},{64,32},{80,48},{96,64},{112,80},{1... | collective-permute-start | bytes 786440 | tf_op jit(solution)/shard_map/ppermute | solution.py:34
  157.8 26.0 %collective-permute-start.28 = (bf16[512,256]{1,0:T(8,128)(2,1)}, bf16[512,256]{1,0:T(8,128)(2,1)S(1)}, u32[]{:S(2)}, u32[]{:S(2)}) collective-permute-start(bf16[512,256]{1,0:T(8,128)(2,1)} %get-tuple-element.7), channel_id=1, source_target_pairs={{0,64},{16,80},{32,96},{48,112},{64,0},{80,16},{96,32},{112,48},{1... | collective-permute-start | bytes 786440 | tf_op jit(solution)/shard_map/ppermute | solution.py:34
  164.4 7.8 %collective-permute-start.13 = (bf16[160,1024]{1,0:T(8,128)(2,1)S(1)}, bf16[160,1024]{1,0:T(8,128)(2,1)S(1)}, u32[]{:S(2)}, u32[]{:S(2)}) collective-permute-start(bf16[160,1024]{1,0:T(8,128)(2,1)S(1)} %slice_bitcast_fusion.15), channel_id=1, source_target_pairs={{0,2},{1,3},{2,0},{3,1},{4,6},{5,7},{6,4},{7,5},{8,10},{9,11},{10,... | collective-permute-start | bytes 983048 | tf_op jit(solution)/shard_map/ppermute | solution.py:27
  164.7 8.7 %collective-permute-start.15 = (bf16[176,1024]{1,0:T(8,128)(2,1)S(1)}, bf16[176,1024]{1,0:T(8,128)(2,1)S(1)}, u32[]{:S(2)}, u32[]{:S(2)}) collective-permute-start(bf16[176,1024]{1,0:T(8,128)(2,1)S(1)} %get-tuple-element.23), channel_id=1, source_target_pairs={{0,4},{1,5},{2,6},{3,7},{4,8},{5,9},{6,10},{7,11},{8,12},{9,13},{1... | collective-permute-start | bytes 1081352 | tf_op jit(solution)/shard_map/ppermute | solution.py:27
  172.2 8.7 %collective-permute-start.18 = (bf16[176,1024]{1,0:T(8,128)(2,1)S(1)}, bf16[176,1024]{1,0:T(8,128)(2,1)S(1)}, u32[]{:S(2)}, u32[]{:S(2)}) collective-permute-start(bf16[176,1024]{1,0:T(8,128)(2,1)S(1)} %get-tuple-element.25), channel_id=1, source_target_pairs={{0,12},{1,13},{2,14},{3,15},{4,0},{5,1},{6,2},{7,3},{8,4},{9,5},{1... | collective-permute-start | bytes 1081352 | tf_op jit(solution)/shard_map/ppermute | solution.py:27
  173.3 26.7 %collective-permute-start.14 = (bf16[512,1024]{1,0:T(8,128)(2,1)}, bf16[512,1024]{1,0:T(8,128)(2,1)}, u32[]{:S(2)}, u32[]{:S(2)}) collective-permute-start(bf16[512,1024]{1,0:T(8,128)(2,1)} %pad_maximum_fusion.6), channel_id=1, source_target_pairs={{0,4},{1,5},{2,6},{3,7},{4,8},{5,9},{6,10},{7,11},{8,12},{9,13},{1... | collective-permute-start | bytes 3145736 | tf_op jit(solution)/shard_map/ppermute | solution.py:27
  182.2 21.3 %collective-permute-start.16 = (bf16[512,1024]{1,0:T(8,128)(2,1)}, bf16[512,1024]{1,0:T(8,128)(2,1)}, u32[]{:S(2)}, u32[]{:S(2)}) collective-permute-start(bf16[512,1024]{1,0:T(8,128)(2,1)} %pad_maximum_fusion.7), channel_id=1, source_target_pairs={{0,2},{1,3},{2,0},{3,1},{4,6},{5,7},{6,4},{7,5},{8,10},{9,11},{10,... | collective-permute-start | bytes 3145736 | tf_op jit(solution)/shard_map/ppermute | solution.py:27
  183.9 22.8 %collective-permute-start.19 = (bf16[512,1024]{1,0:T(8,128)(2,1)}, bf16[512,1024]{1,0:T(8,128)(2,1)}, u32[]{:S(2)}, u32[]{:S(2)}) collective-permute-start(bf16[512,1024]{1,0:T(8,128)(2,1)} %pad_maximum_fusion.9), channel_id=1, source_target_pairs={{0,12},{1,13},{2,14},{3,15},{4,0},{5,1},{6,2},{7,3},{8,4},{9,5},{1... | collective-permute-start | bytes 3145736 | tf_op jit(solution)/shard_map/ppermute | solution.py:27
  185.3 7.9 %collective-permute-start.29 = (bf16[512,256]{1,0:T(8,128)(2,1)}, bf16[512,256]{1,0:T(8,128)(2,1)}, u32[]{:S(2)}, u32[]{:S(2)}) collective-permute-start(bf16[512,256]{1,0:T(8,128)(2,1)} %get-tuple-element.7), channel_id=1, source_target_pairs={{0,32},{16,48},{32,64},{48,80},{64,96},{80,112},{96,0},{112,16},{1... | collective-permute-start | bytes 786440 | tf_op jit(solution)/shard_map/ppermute | solution.py:34
  200.0 9.8 %copy-start.1 = (bf16[4,512,1024]{2,1,0:T(8,128)(2,1)}, bf16[4,512,1024]{2,1,0:T(8,128)(2,1)S(1)}, u32[]{:S(2)}) copy-start(bf16[4,512,1024]{2,1,0:T(8,128)(2,1)S(1)} %shard_map.142) | copy-start | bytes 12582916
  210.8 30.2 %collective-permute-start.21 = (bf16[512,1024]{1,0:T(8,128)(2,1)}, bf16[512,1024]{1,0:T(8,128)(2,1)}, u32[]{:S(2)}, u32[]{:S(2)}) collective-permute-start(bf16[512,1024]{1,0:T(8,128)(2,1)} %pad_maximum_fusion.11), channel_id=1, source_target_pairs={{0,2},{1,3},{2,0},{3,1},{4,6},{5,7},{6,4},{7,5},{8,10},{9,11},{10,... | collective-permute-start | bytes 3145736 | tf_op jit(solution)/shard_map/ppermute | solution.py:27
  212.7 28.3 %collective-permute-start.20 = (bf16[512,1024]{1,0:T(8,128)(2,1)}, bf16[512,1024]{1,0:T(8,128)(2,1)}, u32[]{:S(2)}, u32[]{:S(2)}) collective-permute-start(bf16[512,1024]{1,0:T(8,128)(2,1)} %pad_maximum_fusion.10), channel_id=1, source_target_pairs={{0,12},{1,13},{2,14},{3,15},{4,0},{5,1},{6,2},{7,3},{8,4},{9,5},{1... | collective-permute-start | bytes 3145736 | tf_op jit(solution)/shard_map/ppermute | solution.py:27
  213.9 27.2 %collective-permute-start.17 = (bf16[512,1024]{1,0:T(8,128)(2,1)}, bf16[512,1024]{1,0:T(8,128)(2,1)S(1)}, u32[]{:S(2)}, u32[]{:S(2)}) collective-permute-start(bf16[512,1024]{1,0:T(8,128)(2,1)} %pad_maximum_fusion.8), channel_id=1, source_target_pairs={{0,4},{1,5},{2,6},{3,7},{4,8},{5,9},{6,10},{7,11},{8,12},{9,13},{1... | collective-permute-start | bytes 3145736 | tf_op jit(solution)/shard_map/ppermute | solution.py:27
  (11 other events, 41.0 us)
